TPU v7x, 32 devices: a whole 2x2x4 slice. The times are simulated.
32 devices in a mesh: groups: 2 (over y), neuron: 4 (over z), req: 4 (over x, core).
Axes of the slice: x: 2, y: 2, z: 4, core: 2. Of those that a mesh axis runs over, the one named last changes fastest.
Arguments:
- hidden0: bfloat16 [32, 8, 6144], P(('groups', 'neuron', 'req')), parts along dimension 0, may hold values from -6 to 6
- embeds: bfloat16 [2, 32, 8, 6144], P(None, ('groups', 'neuron', 'req')), parts along dimension 1, may hold values from -6 to 6
- parents: int32 [2, 32, 8], P(None, ('groups', 'neuron', 'req')), parts along dimension 1, may hold values from 0 to 7
- active: int32 [2, 32, 8, 38], P(None, ('groups', 'neuron', 'req')), parts along dimension 1, may hold values from 0 to 383, as said below
- verify_row: int32 [32], P(('groups', 'neuron', 'req')), parts along dimension 0, may hold values from 0 to 7
- norm_gain: float32 [6144], replicated, may hold values from 0.5 to 1.5
- norm_shift: float32 [6144], replicated, may hold values from -3 to 3
- weight_in: bfloat16 [6144, 49152], P(None, ('neuron', 'req')), may hold values from -0.078125 to 0.078125
- bias_in: float32 [49152], P(('neuron', 'req')), may hold values from -4 to 4
- weight_out: bfloat16 [49152, 6144], P(('neuron', 'req')), may hold values from -0.078125 to 0.078125
- bias_out: float32 [6144], replicated, may hold values from -4 to 4
Outputs:
- draft: bfloat16 [32, 8, 6144], P(('groups', 'neuron', 'req')), parts along dimension 0
- verified: bfloat16 [32, 6144], P(('groups', 'neuron', 'req')), parts along dimension 0
There are 2 independent parts, one for each index of `groups`. A program takes and returns all parts, laid end to end along the dimension named above; an argument that names none is the same for every part. Nothing has to cross between parts.
Inputs may be any that keep to these rules, and one draw needn't show every extreme that they name: For each depth, a row's 38 entries are distinct block numbers. Take the 8 rows held by one device. For every device i, the neuron blocks that device i holds (numbers i * 24 to (i + 1) * 24 - 1) appear in the active lists of at most 8 of those rows, and some device i reaches exactly 8.
All inputs are finite; a program needn't handle non-finite values.
Results may differ from a plain program's by a relative error of at most 0.0055.
Values may be sent and summed in bfloat16 or wider, within the bound.
A program may use at most 192 MiB of HBM per device.

v0:
```python
import jax
import jax.numpy as jnp
from jax import lax
from jax.sharding import PartitionSpec as P

BS = 128
DEPTHS = 2


norm_eps = 1e-05


def normalize(values, norm_gain, norm_shift):
    row_mean = jnp.mean(values, axis=-1, keepdims=True)
    centered = values - row_mean
    row_var = jnp.mean(centered * centered, axis=-1, keepdims=True)
    return (centered * lax.rsqrt(row_var + norm_eps) * norm_gain + norm_shift).astype(jnp.bfloat16)


def block_work(pieces, weight_in, bias_in, weight_out):
    incoming, block_tags = pieces
    sources, slots, features = incoming.shape
    blk_dev = block_tags.shape[2]
    preact = (
        jnp.einsum("sck,kn->scn", incoming, weight_in, preferred_element_type=jnp.float32) + bias_in
    )
    masked = (
        jax.nn.relu(preact).reshape(sources, slots, blk_dev, BS)
        * block_tags.astype(jnp.float32)[:, :, :, None]
    )
    hidden = masked.reshape(sources, slots, blk_dev * BS).astype(jnp.bfloat16)
    return jnp.einsum("scn,nk->sck", hidden, weight_out, preferred_element_type=jnp.float32).astype(
        jnp.bfloat16
    )


def body(
    hidden0,
    embeds,
    parents,
    active,
    verify_row,
    norm_gain,
    norm_shift,
    weight_in,
    bias_in,
    weight_out,
    bias_out,
):
    req_dev, frontier, features = hidden0.shape
    active_count = active.shape[3]
    row_count = req_dev * frontier
    neurons = lax.axis_size("neuron")
    req_count = lax.axis_size("req")
    shards = neurons * req_count
    blk_dev = weight_in.shape[1] // BS
    rounds = (row_count * active_count + shards - 1) // shards
    capacity = min(row_count, rounds)
    states = hidden0.astype(jnp.float32)
    for depth_step in range(DEPTHS):
        picked = jnp.take_along_axis(states, parents[depth_step][:, :, None], axis=1)
        pre_state = picked + embeds[depth_step].astype(jnp.float32)
        normed = normalize(pre_state, norm_gain, norm_shift)
        flat_rows = normed.reshape(row_count, features)
        block_list = active[depth_step].reshape(row_count, active_count)
        holder = block_list // blk_dev
        touched = jnp.any(
            holder[:, :, None] == jnp.arange(shards, dtype=jnp.int32)[None, None, :], axis=1
        )
        blockmask = jnp.any(
            block_list[:, :, None] == jnp.arange(shards * blk_dev, dtype=jnp.int32)[None, None, :],
            axis=1,
        )
        blockmask = blockmask.reshape(row_count, shards, blk_dev).astype(jnp.float32)
        hit_count = touched.astype(jnp.int32)
        slot_index = jnp.cumsum(hit_count, axis=0) - hit_count
        selector = touched.T[:, None, :] & (
            slot_index.T[:, None, :] == jnp.arange(capacity, dtype=jnp.int32)[None, :, None]
        )
        picker = selector.astype(jnp.bfloat16)
        outgoing = jnp.einsum(
            "dcr,rk->dck", picker, flat_rows, preferred_element_type=jnp.float32
        ).astype(jnp.bfloat16)
        block_tags = jnp.einsum("dcr,rdj->dcj", selector.astype(jnp.float32), blockmask).astype(
            jnp.bfloat16
        )
        returned = lax.all_to_all(
            block_work(
                (
                    lax.all_to_all(
                        outgoing, ("neuron", "req"), split_axis=0, concat_axis=0, tiled=True
                    ),
                    lax.all_to_all(
                        block_tags, ("neuron", "req"), split_axis=0, concat_axis=0, tiled=True
                    ),
                ),
                weight_in,
                bias_in,
                weight_out,
            ),
            ("neuron", "req"),
            split_axis=0,
            concat_axis=0,
            tiled=True,
        )
        combined = jnp.einsum("dcr,dck->rk", picker, returned, preferred_element_type=jnp.float32)
        states = pre_state + (combined + bias_out).reshape(req_dev, frontier, features)
    verify_in = jnp.take_along_axis(normed, verify_row[:, None, None], axis=1)[:, 0]
    verify_base = jnp.take_along_axis(pre_state, verify_row[:, None, None], axis=1)[:, 0]
    preact = (
        jnp.dot(
            lax.all_gather(verify_in, ("neuron", "req"), axis=0, tiled=True),
            weight_in,
            preferred_element_type=jnp.float32,
        )
        + bias_in
    )
    hidden_all = jax.nn.relu(preact).astype(jnp.bfloat16)
    dense_sum = lax.psum_scatter(
        jnp.dot(hidden_all, weight_out, preferred_element_type=jnp.float32),
        ("neuron", "req"),
        scatter_dimension=0,
        tiled=True,
    )
    verified = (verify_base + bias_out + dense_sum).astype(jnp.bfloat16)
    return (states.astype(jnp.bfloat16), verified)


def solution(mesh):
    return jax.shard_map(
        body,
        mesh=mesh,
        in_specs=(
            P(("groups", "neuron", "req"), None, None),
            P(None, ("groups", "neuron", "req"), None, None),
            P(None, ("groups", "neuron", "req"), None),
            P(None, ("groups", "neuron", "req"), None, None),
            P(("groups", "neuron", "req")),
            P(),
            P(),
            P(None, ("neuron", "req")),
            P(("neuron", "req")),
            P(("neuron", "req"), None),
            P(),
        ),
        out_specs=(
            P(("groups", "neuron", "req"), None, None),
            P(("groups", "neuron", "req"), None),
        ),
        check_vma=False,
    )
```

profile of v0, /device:TPU:0, one launch (start us, length us, event | category | flops | bytes accessed | tf_op | source)
XLA Modules:
  0.0 365.7 jit_solution(15912887324861041570)
XLA Ops:
  7.2 0.8 add_select_fusion
  8.0 0.7 slice_bitcast_fusion
  8.7 0.4 fusion.68
  9.1 0.1 copy.37
  9.3 0.1 fusion.53
  9.4 0.1 reshape.228
  9.5 0.8 convolution_convert_fusion.3
  10.3 7.4 %all-to-all-start.1 = ((bf16[16,8,24]{2,1,0:T(8,128)(2,1)}), bf16[16,8,24]{2,1,0:T(8,128)(2,1)S(1)}, u32[]{:S(2)}, u32[]{:S(2)}) async-start(bf16[16,8,24]{2,1,0:T(8,128)(2,1)} %convolution_convert_fusion.3), calls=%async_computation.1 | async-start | bytes 65536 | tf_op jit(solution)/shard_map/all_to_all | solution.py:93
  17.6 0.7 fusion.79
  18.3 0.7 and_bitcast_fusion
  19.0 0.9 bitcast_convert_fusion
  19.9 0.6 gather_fusion
  20.6 0.2 fusion.82
  20.8 0.2 multiply_reduce_fusion.1
  21.1 1.8 convolution_convert_fusion.1
  22.8 1.4 all-to-all-done.1
  24.3 4.7 %all-to-all-start = ((bf16[16,8,6144]{2,1,0:T(8,128)(2,1)}), bf16[16,8,6144]{2,1,0:T(8,128)(2,1)S(1)}, u32[]{:S(2)}, u32[]{:S(2)}) async-start(bf16[16,8,6144]{2,1,0:T(8,128)(2,1)} %convolution_convert_fusion.1), calls=%async_computation | async-start | bytes 3145728 | tf_op jit(solution)/shard_map/all_to_all | solution.py:90
  29.0 0.1 copy.41
  29.1 31.9 %all-to-all-done = bf16[16,8,6144]{2,1,0:T(8,128)(2,1)S(1)} async-done(((bf16[16,8,6144]{2,1,0:T(8,128)(2,1)}), bf16[16,8,6144]{2,1,0:T(8,128)(2,1)S(1)}, u32[]{:S(2)}, u32[]{:S(2)}) %all-to-all-start) | async-done | bytes 1572896 | tf_op jit(solution)/shard_map/all_to_all | solution.py:90
  61.0 14.5 %fusion.43 = bf16[16,8,3072]{2,1,0:T(8,128)(2,1)S(1)} fusion(bf16[16,8,6144]{2,1,0:T(8,128)(2,1)S(1)} %all-to-all-done, bf16[6144,3072]{1,0:T(8,128)(2,1)} %param.20, f32[16,8,24]{1,2,0:T(8,128)S(1)} %copy.41, f32[3072]{0:T(1024)S(1)} %copy-done.1), kind=kOutput, calls=%fused_computation.31 | convolution fusion | flops 4833411072 | bytes 40132608 | tf_op jit(solution)/shard_map/sck,kn->scn/dot_general | solution.py:25
  75.5 14.8 %fusion.8 = bf16[16,8,6144]{2,0,1:T(8,128)(2,1)S(1)} fusion(bf16[3072,6144]{1,0:T(8,128)(2,1)} %param.22, bf16[16,8,3072]{2,1,0:T(8,128)(2,1)S(1)} %fusion.43), kind=kOutput, calls=%fused_computation.10 | convolution fusion | flops 4832624640 | bytes 40108032 | tf_op jit(solution)/shard_map/scn,nk->sck/dot_general | solution.py:32
  90.3 2.0 copy.43
  92.3 9.2 %all-to-all-start.2 = ((bf16[16,8,6144]{2,1,0:T(8,128)(2,1)}), bf16[16,8,6144]{2,1,0:T(8,128)(2,1)S(1)}, u32[]{:S(2)}, u32[]{:S(2)}) async-start(bf16[16,8,6144]{2,1,0:T(8,128)(2,1)} %copy.43), calls=%async_computation.2 | async-start | bytes 3145728 | tf_op jit(solution)/shard_map/all_to_all | solution.py:87
  101.6 0.1 copy.45
  101.8 0.1 fusion.54
  101.9 0.1 reshape.231
  102.0 0.8 convolution_convert_fusion.2
  102.8 30.7 %all-to-all-done.2 = bf16[16,8,6144]{2,1,0:T(8,128)(2,1)S(1)} async-done(((bf16[16,8,6144]{2,1,0:T(8,128)(2,1)}), bf16[16,8,6144]{2,1,0:T(8,128)(2,1)S(1)}, u32[]{:S(2)}, u32[]{:S(2)}) %all-to-all-start.2) | async-done | bytes 1572896 | tf_op jit(solution)/shard_map/all_to_all | solution.py:87
  133.5 9.1 %all-to-all-start.4 = ((bf16[16,8,24]{2,1,0:T(8,128)(2,1)}), bf16[16,8,24]{2,1,0:T(8,128)(2,1)S(1)}, u32[]{:S(2)}, u32[]{:S(2)}) async-start(bf16[16,8,24]{2,1,0:T(8,128)(2,1)} %convolution_convert_fusion.2), calls=%async_computation.4 | async-start | bytes 65536 | tf_op jit(solution)/shard_map/all_to_all | solution.py:93
  142.6 1.0 fusion.20
  143.6 0.6 gather_fusion.1
  144.2 0.2 fusion.83
  144.5 0.2 multiply_reduce_fusion
  144.7 0.1 add_convert_fusion
  144.8 1.7 convolution_convert_fusion
  146.5 2.7 all-to-all-done.4
  149.3 3.7 %all-to-all-start.3 = ((bf16[16,8,6144]{2,1,0:T(8,128)(2,1)}), bf16[16,8,6144]{2,1,0:T(8,128)(2,1)S(1)}, u32[]{:S(2)}, u32[]{:S(2)}) async-start(bf16[16,8,6144]{2,1,0:T(8,128)(2,1)} %convolution_convert_fusion), calls=%async_computation.3 | async-start | bytes 3145728 | tf_op jit(solution)/shard_map/all_to_all | solution.py:90
  153.6 0.6 dynamic-slice.8
  154.2 0.1 copy.49
  154.4 43.5 %all-gather = bf16[16,1,6144]{2,1,0:T(2,128)(2,1)S(1)} all-gather(bf16[1,1,6144]{2,1,0:T(2,128)(2,1)S(1)} %broadcast_select_fusion), channel_id=2, replica_groups=mesh['groups'=2,'neuron'=4,'req'=4] {'neuron','req'}, dimensions={0}, use_global_device_ids=true | all-gather | bytes 208896 | tf_op jit(solution)/shard_map/all_gather | solution.py:112
  197.9 14.5 %fusion.40 = bf16[16,8,3072]{2,1,0:T(8,128)(2,1)S(1)} fusion(bf16[16,8,6144]{2,1,0:T(8,128)(2,1)S(1)} %all-to-all-done.3, bf16[6144,3072]{1,0:T(8,128)(2,1)} %param.20, f32[16,8,24]{1,2,0:T(8,128)S(1)} %copy.49, f32[3072]{0:T(1024)S(1)} %copy-done.1), kind=kOutput, calls=%fused_computation.30 | convolution fusion | flops 4833411072 | bytes 40132608 | tf_op jit(solution)/shard_map/sck,kn->scn/dot_general | solution.py:25
  212.4 14.8 %fusion.11 = bf16[16,8,6144]{2,0,1:T(8,128)(2,1)S(1)} fusion(bf16[3072,6144]{1,0:T(8,128)(2,1)} %param.22, bf16[16,8,3072]{2,1,0:T(8,128)(2,1)S(1)} %fusion.40), kind=kOutput, calls=%fused_computation.11 | convolution fusion | flops 4832624640 | bytes 40108032 | tf_op jit(solution)/shard_map/scn,nk->sck/dot_general | solution.py:32
  227.1 2.0 copy.51
  229.2 6.9 %all-to-all-start.5 = ((bf16[16,8,6144]{2,1,0:T(8,128)(2,1)}), bf16[16,8,6144]{2,1,0:T(8,128)(2,1)S(1)}, u32[]{:S(2)}, u32[]{:S(2)}) async-start(bf16[16,8,6144]{2,1,0:T(8,128)(2,1)} %copy.51), calls=%async_computation.5 | async-start | bytes 3145728 | tf_op jit(solution)/shard_map/all_to_all | solution.py:87
  236.2 27.1 %fusion.48 = f32[16,6144]{1,0:T(8,128)} fusion(bf16[3072,6144]{1,0:T(8,128)(2,1)} %param.22, bf16[6144,3072]{1,0:T(8,128)(2,1)} %param.20, bf16[16,1,6144]{2,1,0:T(2,128)(2,1)S(1)} %all-gather, f32[3072]{0:T(1024)S(1)} %copy-done.1), kind=kOutput, calls=%fused_computation.35 | convolution fusion | flops 1208107008 | bytes 76099584 | tf_op jit(solution)/shard_map/dot_general | solution.py:120
  263.3 91.8 %all-reduce.3.cloned.1.call-done = f32[16,6144]{1,0:T(8,128)} async-done(((f32[16,6144]{1,0:T(8,128)}), f32[16,6144]{1,0:T(8,128)}) %all-reduce.3.cloned.1.call-update) | async-done | bytes 393232
  355.1 2.1 fusion.74
  357.3 1.6 fusion.21
  (35 shorter events, 0.5 us)
Async XLA Ops:
  7.2 13.4 %copy-start = (bf16[2,1,8,6144]{3,2,1,0:T(8,128)(2,1)S(1)}, bf16[2,1,8,6144]{3,2,1,0:T(8,128)(2,1)}, u32[]{:S(2)}) copy-start(bf16[2,1,8,6144]{3,2,1,0:T(8,128)(2,1)} %param.14) | copy-start | bytes 589828
  7.2 13.9 %copy-start.3 = (f32[6144]{0:T(1024)S(1)}, f32[6144]{0:T(1024)}, u32[]{:S(2)}) copy-start(f32[6144]{0:T(1024)} %param.18) | copy-start | bytes 73732
  7.2 13.9 %copy-start.2 = (f32[6144]{0:T(1024)S(1)}, f32[6144]{0:T(1024)}, u32[]{:S(2)}) copy-start(f32[6144]{0:T(1024)} %param.19) | copy-start | bytes 73732
  10.3 14.0 %all-to-all-start.1 = ((bf16[16,8,24]{2,1,0:T(8,128)(2,1)}), bf16[16,8,24]{2,1,0:T(8,128)(2,1)S(1)}, u32[]{:S(2)}, u32[]{:S(2)}) async-start(bf16[16,8,24]{2,1,0:T(8,128)(2,1)} %convolution_convert_fusion.3), calls=%async_computation.1 | async-start | bytes 65536 | tf_op jit(solution)/shard_map/all_to_all | solution.py:93
  22.8 38.1 %copy-start.1 = (f32[3072]{0:T(1024)S(1)}, f32[3072]{0:T(1024)}, u32[]{:S(2)}) copy-start(f32[3072]{0:T(1024)} %param.21) | copy-start | bytes 36868
  24.3 36.7 %all-to-all-start = ((bf16[16,8,6144]{2,1,0:T(8,128)(2,1)}), bf16[16,8,6144]{2,1,0:T(8,128)(2,1)S(1)}, u32[]{:S(2)}, u32[]{:S(2)}) async-start(bf16[16,8,6144]{2,1,0:T(8,128)(2,1)} %convolution_convert_fusion.1), calls=%async_computation | async-start | bytes 3145728 | tf_op jit(solution)/shard_map/all_to_all | solution.py:90
  92.3 50.3 %copy-start.4 = (f32[6144]{0:T(1024)S(1)}, f32[6144]{0:T(1024)}, u32[]{:S(2)}) copy-start(f32[6144]{0:T(1024)} %param.23) | copy-start | bytes 73732
  92.3 41.2 %all-to-all-start.2 = ((bf16[16,8,6144]{2,1,0:T(8,128)(2,1)}), bf16[16,8,6144]{2,1,0:T(8,128)(2,1)S(1)}, u32[]{:S(2)}, u32[]{:S(2)}) async-start(bf16[16,8,6144]{2,1,0:T(8,128)(2,1)} %copy.43), calls=%async_computation.2 | async-start | bytes 3145728 | tf_op jit(solution)/shard_map/all_to_all | solution.py:87
  133.5 15.7 %all-to-all-start.4 = ((bf16[16,8,24]{2,1,0:T(8,128)(2,1)}), bf16[16,8,24]{2,1,0:T(8,128)(2,1)S(1)}, u32[]{:S(2)}, u32[]{:S(2)}) async-start(bf16[16,8,24]{2,1,0:T(8,128)(2,1)} %convolution_convert_fusion.2), calls=%async_computation.4 | async-start | bytes 65536 | tf_op jit(solution)/shard_map/all_to_all | solution.py:93
  146.5 7.1 %copy-start.5 = (u32[32]{0:T(128)S(1)}, u32[32]{0:T(128)}, u32[]{:S(2)}) copy-start(u32[32]{0:T(128)} %constant.122) | copy-start | bytes 388
  149.3 48.6 %all-to-all-start.3 = ((bf16[16,8,6144]{2,1,0:T(8,128)(2,1)}), bf16[16,8,6144]{2,1,0:T(8,128)(2,1)S(1)}, u32[]{:S(2)}, u32[]{:S(2)}) async-start(bf16[16,8,6144]{2,1,0:T(8,128)(2,1)} %convolution_convert_fusion), calls=%async_computation.3 | async-start | bytes 3145728 | tf_op jit(solution)/shard_map/all_to_all | solution.py:90
  229.2 128.1 %all-to-all-start.5 = ((bf16[16,8,6144]{2,1,0:T(8,128)(2,1)}), bf16[16,8,6144]{2,1,0:T(8,128)(2,1)S(1)}, u32[]{:S(2)}, u32[]{:S(2)}) async-start(bf16[16,8,6144]{2,1,0:T(8,128)(2,1)} %copy.51), calls=%async_computation.5 | async-start | bytes 3145728 | tf_op jit(solution)/shard_map/all_to_all | solution.py:87
  236.1 119.0 %all-reduce.3.cloned.1.call-start = ((), (), s32[]{:S(2)}) async-start(), calls=%async_computation.6 | async-start | bytes 786432
Sparse Core Ops, SparseCore 0:
  263.4 91.6 all-reduce.2
where the time goes:
time: 366 us
  waiting for transfers between devices  159 us (43%)
  matrix products  93.2 us (25%)
  blocking collectives  43.5 us (12%)
  starting transfers between devices  41.1 us (11%)
  between operations  15 us (4%)
  local copies, waits for them, and re-layouts  7.36 us (2%)
  other arithmetic  7.04 us (2%)
    unnamed x2, waiting for transfers between devices  91.8 us
    all_gather x1, blocking collectives, body(): lax.all_gather(verify_in, ('neuron', 'req'), axis=0, tiled=True)  43.5 us
    all_to_all x2, waiting for transfers between devices, body(): lax.all_to_all(outgoing, ('neuron', 'req'), split_axis=0, concat_axis=0,...  31.9 us
    all_to_all x2, waiting for transfers between devices, body(): lax.all_to_all(block_work((lax.all_to_all(outgoing, ('neuron', 'req'), sp...  30.7 us
    dot_general x2, matrix products, block_work(): jnp.einsum('scn,nk->sck', hidden, weight_out, preferred_element_type=jnp....  29.5 us
    dot_general x2, matrix products, block_work(): jnp.einsum('sck,kn->scn', incoming, weight_in, preferred_element_type=jnp...  29 us
    dot_general x1, matrix products, body(): jnp.dot(hidden_all, weight_out, preferred_element_type=jnp.float32)  27.1 us
    all_to_all x2, starting transfers between devices, body(): lax.all_to_all(block_tags, ('neuron', 'req'), split_axis=0, concat_axis=0...  16.5 us
  transfers between devices with their start and end apart: 7, of which 5 were waited for; matrix products, arithmetic and copies ran while one was open for 11% of the time, Pallas kernels for 0%

commit v1 on v0

v1 whole, which is shorter than its diff:
```python
import functools

import jax
import jax.numpy as jnp
from jax import lax
from jax.experimental import pallas as pl
from jax.experimental.pallas import tpu as pltpu
from jax.sharding import PartitionSpec as P

BS = 128
DEPTHS = 2
CORES = 2
CHUNK = 1024
SUB = CHUNK // 2
SLOTS = 4
ROWS = 8
VMEM_LIMIT = 63 * 1024 * 1024

norm_eps = 1e-05
MESH = pl.DeviceIdType.MESH
F32 = jnp.float32
BF16 = jnp.bfloat16


def kernel(
    nz,
    nx,
    hidden_ref,
    embeds_ref,
    parents_ref,
    active_ref,
    vrow_ref,
    gain_ref,
    shift_ref,
    win_hbm,
    bin_ref,
    wout_hbm,
    bout_ref,
    draft_ref,
    verified_ref,
    win_v,
    wout_v,
    xbuf,
    mbuf,
    mask_v,
    flag_v,
    hid,
    ybuf,
    rc,
    rx,
    rz,
    pre_v,
    state_v,
    ver_v,
    vline,
    win_sem,
    wout_sem,
    ag_recv,
    ag_zs,
    ag_xs,
    ag_cs,
    rc_send,
    rc_recv,
    rx_send,
    rx_recv,
    rz_send,
    rz_recv,
):
    shards = CORES * nx * nz
    features = hidden_ref.shape[2]
    half = features // 2
    tiles, _, ht = win_v.shape
    nblk = mask_v.shape[1]
    blk_tile = ht // BS
    chunks = features // CHUNK
    outs_dev = features // SUB
    all_rows = shards * ROWS

    g = lax.axis_index("groups")
    z = lax.axis_index("neuron")
    req = lax.axis_index("req")
    x = req // CORES
    c = req % CORES
    me = z * (nx * CORES) + req
    oc = 1 - c

    def dev(zz, xx, cc):
        return (g, zz, xx * CORES + cc)

    def zpeer(d):
        out, bit = z, 1
        while bit < nz:
            if d & bit:
                out = out + bit - 2 * bit * ((z // bit) % 2)
            bit *= 2
        return out

    zs = [zpeer(d) for d in range(nz)]
    xs = [(x + e) % nx for e in range(nx)]

    barrier = pltpu.get_barrier_semaphore()
    peers = [dev(zs[d], x, c) for d in range(1, nz)]
    peers += [dev(z, xs[e], c) for e in range(1, nx)]
    peers += [dev(z, x, oc)]
    for peer in peers:
        pl.semaphore_signal(barrier, inc=1, device_id=peer, device_id_type=MESH)

    def win_copy(t):
        return pltpu.make_async_copy(
            win_hbm.at[:, pl.ds(pl.multiple_of(t * ht, ht), ht)], win_v.at[t], win_sem.at[t]
        )

    def wout_copy(k):
        col = pl.multiple_of((k % outs_dev) * SUB, SUB)
        slot = k % SLOTS
        return pltpu.make_async_copy(
            wout_hbm.at[:, pl.ds(col, SUB)], wout_v.at[slot], wout_sem.at[slot]
        )

    for t in range(tiles):
        win_copy(t).start()
    for k in range(SLOTS):
        wout_copy(k).start()

    block_ids = lax.broadcasted_iota(jnp.int32, (ROWS, nblk), 1)
    row_ids = lax.broadcasted_iota(jnp.int32, (ROWS, BS), 0)
    flag = (row_ids == vrow_ref[...]).astype(F32)
    sides = []
    for depth in range(DEPTHS):
        listed = active_ref[depth, 0]
        member = jnp.zeros((ROWS, nblk), F32)
        for j in range(listed.shape[1]):
            member = jnp.where(listed[:, j : j + 1] == block_ids, 1.0, member)
        sides.append(jnp.concatenate([member, flag], axis=1))
    mbuf[c, x, z] = jnp.concatenate(sides, axis=0).astype(BF16)

    def prepare(depth):
        states = hidden_ref[0].astype(F32) if depth == 0 else state_v[...]
        eye_r = lax.broadcasted_iota(jnp.int32, (ROWS, ROWS), 0)
        eye_c = lax.broadcasted_iota(jnp.int32, (ROWS, ROWS), 1)
        par = jnp.sum(
            jnp.where(eye_r == eye_c, jnp.broadcast_to(parents_ref[depth], (ROWS, ROWS)), 0),
            axis=1,
            keepdims=True,
        )
        picked = jnp.zeros((ROWS, features), F32)
        for p in range(ROWS):
            picked = jnp.where(par == p, states[p : p + 1, :], picked)
        pre = picked + embeds_ref[depth, 0].astype(F32)
        pre_v[...] = pre
        centered = pre - jnp.mean(pre, axis=-1, keepdims=True)
        var = jnp.mean(centered * centered, axis=-1, keepdims=True)
        normed = centered * lax.rsqrt(var + norm_eps) * gain_ref[...] + shift_ref[...]
        xbuf[c, x, z] = jnp.concatenate([normed[:, :half], normed[:, half:]], axis=0).astype(BF16)

    def gather(bufs):
        started = []

        def send(i, block, to, send_sem):
            cc, xx, zz = block
            ref = bufs[i][1].at[cc, xx, zz]
            copy = pltpu.make_async_remote_copy(
                src_ref=ref,
                dst_ref=ref,
                send_sem=send_sem,
                recv_sem=ag_recv.at[bufs[i][0], cc, xx, zz],
                device_id=to,
                device_id_type=MESH,
            )
            copy.start()
            started.append(copy)

        def arrived(i, block):
            cc, xx, zz = block
            ref = bufs[i][1].at[cc, xx, zz]
            pltpu.make_async_copy(ref, ref, ag_recv.at[bufs[i][0], cc, xx, zz]).wait()

        many = range(len(bufs))
        for i in many:
            b = bufs[i][0]
            for d in range(1, nz):
                send(i, (c, x, z), dev(zs[d], x, c), ag_zs.at[b, d])
        for d in range(nz):
            for i in many:
                b = bufs[i][0]
                if d > 0:
                    arrived(i, (c, x, zs[d]))
                for e in range(1, nx):
                    send(i, (c, x, zs[d]), dev(z, xs[e], c), ag_xs.at[b, e, d])
                send(i, (c, x, zs[d]), dev(z, x, oc), ag_cs.at[b, 0, d])
        for d in range(nz):
            for e in range(1, nx):
                for i in many:
                    b = bufs[i][0]
                    arrived(i, (c, xs[e], zs[d]))
                    send(i, (c, xs[e], zs[d]), dev(z, x, oc), ag_cs.at[b, e, d])
        for e in range(nx):
            for d in range(nz):
                for i in many:
                    arrived(i, (oc, xs[e], zs[d]))
        for copy in started:
            copy.wait_send()

    def swap_rows():
        @pl.loop(0, CORES * nx)
        def _(i):
            cc, xx = i // nx, i % nx
            for zz in range(0, nz, 2):
                first = xbuf[cc, xx, zz].astype(F32)
                second = xbuf[cc, xx, zz + 1].astype(F32)
                xbuf[cc, xx, zz] = jnp.concatenate([first[:ROWS], second[:ROWS]], axis=0).astype(BF16)
                xbuf[cc, xx, zz + 1] = jnp.concatenate([first[ROWS:], second[ROWS:]], axis=0).astype(BF16)

    def first_projection(depth):
        meta = mbuf[...].astype(F32).reshape(shards, DEPTHS * ROWS, nblk + BS)
        meta = meta[:, depth * ROWS : (depth + 1) * ROWS, :].reshape(all_rows, nblk + BS)
        mask_v[...] = meta[:, :nblk].astype(BF16)
        if depth == DEPTHS - 1:
            flag_v[...] = meta[:, nblk:]

        @pl.loop(0, tiles)
        def _(t):
            if depth == 0:
                win_copy(t).wait()
            pairs = xbuf.reshape(shards // 2, 2, 2 * ROWS, half)
            pre = jnp.dot(
                pairs[:, 0].reshape(all_rows, half), win_v[t, :half, :], preferred_element_type=F32
            )
            pre += jnp.dot(
                pairs[:, 1].reshape(all_rows, half), win_v[t, half:, :], preferred_element_type=F32
            )
            col = pl.ds(pl.multiple_of(t * ht, ht), ht)
            act = jnp.maximum(pre + bin_ref[:, col], 0.0)
            which = lax.broadcasted_iota(jnp.int32, (nblk, ht), 0)
            unit = lax.broadcasted_iota(jnp.int32, (nblk, ht), 1) // BS
            spread = (which == unit + (me * tiles + t) * blk_tile).astype(F32).astype(BF16)
            keep = jnp.dot(mask_v[...], spread, preferred_element_type=F32)
            hid[:all_rows, col] = (act * keep).astype(BF16)
            if depth == DEPTHS - 1:
                wide = jnp.concatenate([flag_v[...]] * blk_tile, axis=1)
                one = jnp.sum((act * wide).reshape(shards, ROWS, ht), axis=1)
                hid[all_rows:, col] = one.astype(BF16)

    def second_projection(depth):
        last = depth == DEPTHS - 1
        width = SUB + BS if last else SUB
        lanes = pl.ds(0, width)
        rows = hid.shape[0] if last else all_rows

        def core_copy(n):
            return pltpu.make_async_remote_copy(
                src_ref=ybuf.at[n, oc, :, :, :, lanes],
                dst_ref=rc.at[n, :, :, :, lanes],
                send_sem=rc_send.at[n],
                recv_sem=rc_recv.at[n],
                device_id=dev(z, x, oc),
                device_id_type=MESH,
            )

        def x_copy(n, e):
            return pltpu.make_async_remote_copy(
                src_ref=ybuf.at[n, c, xs[e], :, :, lanes],
                dst_ref=rx.at[n, e - 1, :, :, lanes],
                send_sem=rx_send.at[n, e],
                recv_sem=rx_recv.at[n, e],
                device_id=dev(z, xs[e], c),
                device_id_type=MESH,
            )

        def z_copy(n, d):
            return pltpu.make_async_remote_copy(
                src_ref=ybuf.at[n, c, x, zs[d], :, lanes],
                dst_ref=rz.at[n, d - 1, :, lanes],
                send_sem=rz_send.at[n, d],
                recv_sem=rz_recv.at[n, d],
                device_id=dev(zs[d], x, c),
                device_id_type=MESH,
            )

        def compute(n):
            slot = []
            for sub in range(2):
                k = depth * outs_dev + n * 2 + sub
                wout_copy(k).wait()
                slot.append(k % SLOTS)
            pieces = jnp.zeros((shards, ROWS, BS), F32)
            place = lax.broadcasted_iota(jnp.int32, (shards, ROWS, BS), 1)
            step = 256
            for q in range(SUB // step):
                cols = slice(q * step, (q + 1) * step)
                parts = []
                for sub in range(2):
                    y = jnp.dot(hid[:rows, :], wout_v[slot[sub], :, cols], preferred_element_type=F32)
                    parts.append(y[:all_rows].reshape(shards, ROWS, step))
                    if last:
                        for r in range(step // BS):
                            spot = (sub * SUB + q * step) // BS + r
                            line = y[all_rows : all_rows + shards, r * BS : (r + 1) * BS]
                            pieces = jnp.where(place == spot, line[:, None, :], pieces)
                packed = jnp.concatenate(parts, axis=1).astype(BF16)
                ybuf[n, :, :, :, :, cols] = packed.reshape(CORES, nx, nz, 2 * ROWS, step)
            if last:
                packed = jnp.concatenate([pieces, jnp.zeros_like(pieces)], axis=1).astype(BF16)
                ybuf[n, :, :, :, :, SUB:] = packed.reshape(CORES, nx, nz, 2 * ROWS, BS)
            core_copy(n).start()
            for sub in range(2):
                k = depth * outs_dev + n * 2 + sub + SLOTS

                @pl.when(k < DEPTHS * outs_dev)
                def _():
                    wout_copy(k).start()

        def add_core(n):
            core_copy(n).wait_recv()
            for xx in range(nx):
                total = ybuf[n, c, xx, :, :, :width].astype(F32) + rc[n, xx, :, :, :width].astype(F32)
                ybuf[n, c, xx, :, :, :width] = total.astype(BF16)
            for e in range(1, nx):
                x_copy(n, e).start()

        def add_x(n):
            total = ybuf[n, c, x, :, :, :width].astype(F32)
            for e in range(1, nx):
                x_copy(n, e).wait_recv()
                total += rx[n, e - 1, :, :, :width].astype(F32)
            ybuf[n, c, x, :, :, :width] = total.astype(BF16)
            for d in range(1, nz):
                z_copy(n, d).start()

        def add_z(n):
            total = ybuf[n, c, x, z, :, :width].astype(F32)
            for d in range(1, nz):
                z_copy(n, d).wait_recv()
                total += rz[n, d - 1, :, :width].astype(F32)
            cols = pl.ds(pl.multiple_of(n * CHUNK, CHUNK), CHUNK)
            rows_out = jnp.concatenate([total[:ROWS, :SUB], total[ROWS:, :SUB]], axis=1)
            state_v[:, cols] = pre_v[:, cols] + (rows_out + bout_ref[:, cols])
            if last:
                ver_v[n] = total[:ROWS, SUB:]

        @pl.loop(0, chunks + 3)
        def _(n):
            @pl.when(n < chunks)
            def _():
                compute(n)

            @pl.when((n >= 1) & (n < chunks + 1))
            def _():
                add_core(n - 1)

            @pl.when((n >= 2) & (n < chunks + 2))
            def _():
                add_x(n - 2)

            @pl.when(n >= 3)
            def _():
                add_z(n - 3)

        @pl.loop(0, chunks)
        def _(n):
            core_copy(n).wait_send()
            for e in range(1, nx):
                x_copy(n, e).wait_send()
            for d in range(1, nz):
                z_copy(n, d).wait_send()

    prepare(0)
    pl.semaphore_wait(barrier, len(peers))
    for depth in range(DEPTHS):
        if depth > 0:
            prepare(depth)
        gather([(0, mbuf), (1, xbuf)] if depth == 0 else [(1, xbuf)])
        swap_rows()
        first_projection(depth)
        second_projection(depth)

    draft_ref[0] = state_v[...].astype(BF16)
    full_ids = lax.broadcasted_iota(jnp.int32, (ROWS, features), 0)
    base = jnp.sum(jnp.where(full_ids == vrow_ref[...], pre_v[...], 0.0), axis=0, keepdims=True)
    for n in range(chunks):
        piece = ver_v[n]
        for r in range(ROWS):
            vline[:, n * CHUNK + r * BS : n * CHUNK + (r + 1) * BS] = piece[r : r + 1, :]
    verified_ref[...] = (base + bout_ref[...] + vline[...]).astype(BF16)


def tile_width(width, most):
    return max(t for t in range(BS, most + 1, BS) if width % t == 0)


def body(
    nz,
    nx,
    hidden0,
    embeds,
    parents,
    active,
    verify_row,
    norm_gain,
    norm_shift,
    weight_in,
    bias_in,
    weight_out,
    bias_out,
):
    features, width = weight_in.shape
    shards = CORES * nx * nz
    rows = shards * ROWS
    nblk = shards * width // BS
    ht = tile_width(width, 512)
    tiles = width // ht
    chunks = features // CHUNK
    vm = pl.BlockSpec(memory_space=pltpu.VMEM)
    hbm = pl.BlockSpec(memory_space=pl.ANY)
    dma = pltpu.SemaphoreType.DMA
    return pl.pallas_call(
        functools.partial(kernel, nz, nx),
        out_shape=(
            jax.ShapeDtypeStruct(hidden0.shape, BF16),
            jax.ShapeDtypeStruct((1, features), BF16),
        ),
        in_specs=[vm, vm, vm, vm, vm, vm, vm, hbm, vm, hbm, vm],
        out_specs=(vm, vm),
        scratch_shapes=[
            pltpu.VMEM((tiles, features, ht), BF16),
            pltpu.VMEM((SLOTS, width, SUB), BF16),
            pltpu.VMEM((CORES, nx, nz, 2 * ROWS, features // 2), BF16),
            pltpu.VMEM((CORES, nx, nz, DEPTHS * ROWS, nblk + BS), BF16),
            pltpu.VMEM((rows, nblk), BF16),
            pltpu.VMEM((rows, BS), F32),
            pltpu.VMEM((rows + shards, width), BF16),
            pltpu.VMEM((chunks, CORES, nx, nz, 2 * ROWS, SUB + BS), BF16),
            pltpu.VMEM((chunks, nx, nz, 2 * ROWS, SUB + BS), BF16),
            pltpu.VMEM((chunks, nx - 1, nz, 2 * ROWS, SUB + BS), BF16),
            pltpu.VMEM((chunks, nz - 1, 2 * ROWS, SUB + BS), BF16),
            pltpu.VMEM((ROWS, features), F32),
            pltpu.VMEM((ROWS, features), F32),
            pltpu.VMEM((chunks, ROWS, BS), F32),
            pltpu.VMEM((1, features), F32),
            dma((tiles,)),
            dma((SLOTS,)),
            dma((2, CORES, nx, nz)),
            dma((2, nz)),
            dma((2, nx, nz)),
            dma((2, nx, nz)),
            dma((chunks,)),
            dma((chunks,)),
            dma((chunks, nx)),
            dma((chunks, nx)),
            dma((chunks, nz)),
            dma((chunks, nz)),
        ],
        compiler_params=pltpu.CompilerParams(
            collective_id=0, has_side_effects=True, vmem_limit_bytes=VMEM_LIMIT
        ),
        cost_estimate=pl.CostEstimate(
            flops=4 * DEPTHS * rows * features * width,
            bytes_accessed=6 * features * width,
            transcendentals=0,
        ),
    )(
        hidden0,
        embeds,
        parents,
        active,
        verify_row.reshape(1, 1),
        norm_gain.reshape(1, -1),
        norm_shift.reshape(1, -1),
        weight_in,
        bias_in.reshape(1, -1),
        weight_out,
        bias_out.reshape(1, -1),
    )


def solution(mesh):
    nz = mesh.shape["neuron"]
    nx = mesh.shape["req"] // CORES
    return jax.shard_map(
        functools.partial(body, nz, nx),
        mesh=mesh,
        in_specs=(
            P(("groups", "neuron", "req"), None, None),
            P(None, ("groups", "neuron", "req"), None, None),
            P(None, ("groups", "neuron", "req"), None),
            P(None, ("groups", "neuron", "req"), None, None),
            P(("groups", "neuron", "req")),
            P(),
            P(),
            P(None, ("neuron", "req")),
            P(("neuron", "req")),
            P(("neuron", "req"), None),
            P(),
        ),
        out_specs=(
            P(("groups", "neuron", "req"), None, None),
            P(("groups", "neuron", "req"), None),
        ),
        check_vma=False,
    )
```

time: 366 us -> 102 us (0.28)
  waiting for transfers between devices: 159 us -> 0 us
  Pallas kernels: 0 us -> 97.9 us
  matrix products: 93.2 us -> 0 us
  blocking collectives: 43.5 us -> 0 us
  starting transfers between devices: 41.1 us -> 0 us
  between operations: 15 us -> 1.29 us
  other arithmetic: 7.04 us -> 0 us
  local copies, waits for them, and re-layouts: 7.36 us -> 2.91 us
    pallas_call x0 -> x1, Pallas kernels: none -> 97.9 us  [body(): pl.pallas_call(functools.partial(kernel, nz, nx), out_shape=(jax.ShapeDty...]
    dot_general x11 -> x0, matrix products: 93.2 us -> none  [the longest x2 29.5 us: block_work(): jnp.einsum('scn,nk->sck', hidden, weight_out, preferred_element_type=jnp....]
    unnamed x2 -> x0, waiting for transfers between devices: 91.8 us -> none
    all_to_all x6 -> x0, waiting for transfers between devices: 66.7 us -> none  [the longest x2 31.9 us: body(): lax.all_to_all(outgoing, ('neuron', 'req'), split_axis=0, concat_axis=0,...]
    all_gather x1 -> x0, blocking collectives: 43.5 us -> none  [body(): lax.all_gather(verify_in, ('neuron', 'req'), axis=0, tiled=True)]
    all_to_all x6 -> x0, starting transfers between devices: 41 us -> none  [the longest x2 16.5 us: body(): lax.all_to_all(block_tags, ('neuron', 'req'), split_axis=0, concat_axis=0...]
    convert_element_type x4 -> x0, local copies, waits for them, and re-layouts: 4.24 us -> none  [the longest x2 4.05 us: block_work(): jnp.einsum('scn,nk->sck', hidden, weight_out, preferred_element_type=jnp....]
  transfers between devices with their start and end apart: 7 -> 0, of which waited for: 5 -> 0; matrix products, arithmetic and copies ran while one was open for 11% -> 0% of each run, Pallas kernels for 0% -> 0%
where the time goes in v1:
time: 102 us
  Pallas kernels  97.9 us (96%)
  local copies, waits for them, and re-layouts  2.91 us (3%)
  between operations  1.29 us (1%)
    pallas_call x1, Pallas kernels, body(): pl.pallas_call(functools.partial(kernel, nz, nx), out_shape=(jax.ShapeDty...  97.9 us
    unnamed x2, local copies, waits for them, and re-layouts  2.91 us

profile of v1, /device:TPU:0, one launch (start us, length us, event | category | flops | bytes accessed | tf_op | source)
XLA Modules:
  0.0 102.1 jit_solution(1933284211212790598)
XLA Ops:
  1.3 97.9 %shard_map.122 = (bf16[1,8,6144]{2,1,0:T(8,128)(2,1)}, bf16[1,6144]{1,0:T(2,128)(2,1)}) custom-call(bf16[1,8,6144]{2,1,0:T(8,128)(2,1)} %hidden_ref.1, bf16[2,1,8,6144]{3,2,1,0:T(8,128)(2,1)} %embeds_ref.1, s32[2,1,8]{2,1,0:T(1,128)} %parents_ref.1, s32[2,1,8,38]{3,2,1,0:T(8,128)} %active_ref.1, s32[1,1]{1,0:T(1,128)} %bitcast.5.vrow_ref, ...), custom_call_target="tpu_custom_call" | custom-call | flops 19327352832 | bytes 113246208 | tf_op jit(solution)/shard_map/pallas_call | solution.py:416
  99.2 1.5 %copy.16 = bf16[1,8,6144]{2,1,0:T(8,128)(2,1)} copy(bf16[1,8,6144]{2,1,0:T(8,128)(2,1)} %get-tuple-element.4) | data formatting | bytes 196608
  100.7 1.4 %copy.17 = bf16[1,6144]{1,0:T(2,128)(2,1)} copy(bf16[1,6144]{1,0:T(2,128)(2,1)} %get-tuple-element.5) | data formatting | bytes 24576

commit v2 on v1

--- a/solution.py
+++ b/solution.py
@@ -13,6 +13,8 @@
 CHUNK = 1024
 SUB = CHUNK // 2
 SLOTS = 4
+LAGS = (1, 3, 5)
+PARTS = 2
 ROWS = 8
 VMEM_LIMIT = 63 * 1024 * 1024
 
@@ -44,6 +46,7 @@
     mbuf,
     mask_v,
     flag_v,
+    acc,
     hid,
     ybuf,
     rc,
@@ -55,7 +58,9 @@
     vline,
     win_sem,
     wout_sem,
-    ag_recv,
+    ag_zr,
+    ag_xr,
+    ag_cr,
     ag_zs,
     ag_xs,
     ag_cs,
@@ -68,8 +73,9 @@
 ):
     shards = CORES * nx * nz
     features = hidden_ref.shape[2]
-    half = features // 2
-    tiles, _, ht = win_v.shape
+    part = features // PARTS
+    half = part // 2
+    tiles, _, ht = acc.shape
     nblk = mask_v.shape[1]
     blk_tile = ht // BS
     chunks = features // CHUNK
@@ -105,9 +111,9 @@
     for peer in peers:
         pl.semaphore_signal(barrier, inc=1, device_id=peer, device_id_type=MESH)
 
-    def win_copy(t):
+    def win_copy(a):
         return pltpu.make_async_copy(
-            win_hbm.at[:, pl.ds(pl.multiple_of(t * ht, ht), ht)], win_v.at[t], win_sem.at[t]
+            win_hbm.at[pl.ds(a * part, part), :], win_v.at[a], win_sem.at[a]
         )
 
     def wout_copy(k):
@@ -117,8 +123,8 @@
             wout_hbm.at[:, pl.ds(col, SUB)], wout_v.at[slot], wout_sem.at[slot]
         )
 
-    for t in range(tiles):
-        win_copy(t).start()
+    for a in range(PARTS):
+        win_copy(a).start()
     for k in range(SLOTS):
         wout_copy(k).start()
 
@@ -151,85 +157,105 @@
         centered = pre - jnp.mean(pre, axis=-1, keepdims=True)
         var = jnp.mean(centered * centered, axis=-1, keepdims=True)
         normed = centered * lax.rsqrt(var + norm_eps) * gain_ref[...] + shift_ref[...]
-        xbuf[c, x, z] = jnp.concatenate([normed[:, :half], normed[:, half:]], axis=0).astype(BF16)
-
-    def gather(bufs):
-        started = []
-
-        def send(i, block, to, send_sem):
-            cc, xx, zz = block
-            ref = bufs[i][1].at[cc, xx, zz]
+        for a in range(PARTS):
+            two = [normed[:, a * part + h * half : a * part + (h + 1) * half] for h in range(2)]
+            xbuf[a, c, x, z] = jnp.concatenate(two, axis=0).astype(BF16)
+
+    def gather_steps(depth):
+        started = [[] for _ in range(PARTS)]
+
+        def refs(a):
+            pairs = [(a + 1, xbuf.at[a])]
+            return [(0, mbuf)] + pairs if depth == 0 and a == 0 else pairs
+
+        def send(a, ref, to, send_sem, recv_sem):
             copy = pltpu.make_async_remote_copy(
                 src_ref=ref,
                 dst_ref=ref,
                 send_sem=send_sem,
-                recv_sem=ag_recv.at[bufs[i][0], cc, xx, zz],
+                recv_sem=recv_sem,
                 device_id=to,
                 device_id_type=MESH,
             )
             copy.start()
-            started.append(copy)
-
-        def arrived(i, block):
-            cc, xx, zz = block
-            ref = bufs[i][1].at[cc, xx, zz]
-            pltpu.make_async_copy(ref, ref, ag_recv.at[bufs[i][0], cc, xx, zz]).wait()
-
-        many = range(len(bufs))
-        for i in many:
-            b = bufs[i][0]
+            started[a].append(copy)
+
+        def arrived(ref, sem):
+            pltpu.make_async_copy(ref, ref, sem).wait()
+
+        def x_send(a, d):
+            for b, buf in refs(a):
+                for e in range(1, nx):
+                    block = buf.at[c, x, zs[d]]
+                    send(a, block, dev(z, xs[e], c), ag_xs.at[b, e, d], ag_xr.at[b, x, zs[d]])
+
+        def own(a):
+            for b, buf in refs(a):
+                for d in range(1, nz):
+                    send(a, buf.at[c, x, z], dev(zs[d], x, c), ag_zs.at[b, d], ag_zr.at[b, z])
+            x_send(a, 0)
+
+        def along_x(a):
             for d in range(1, nz):
-                send(i, (c, x, z), dev(zs[d], x, c), ag_zs.at[b, d])
-        for d in range(nz):
-            for i in many:
-                b = bufs[i][0]
-                if d > 0:
-                    arrived(i, (c, x, zs[d]))
-                for e in range(1, nx):
-                    send(i, (c, x, zs[d]), dev(z, xs[e], c), ag_xs.at[b, e, d])
-                send(i, (c, x, zs[d]), dev(z, x, oc), ag_cs.at[b, 0, d])
-        for d in range(nz):
+                for b, buf in refs(a):
+                    arrived(buf.at[c, x, zs[d]], ag_zr.at[b, zs[d]])
+                x_send(a, d)
+            for b, buf in refs(a):
+                send(a, buf.at[c, x], dev(z, x, oc), ag_cs.at[b, 0], ag_cr.at[b, x])
+
+        def along_core(a):
             for e in range(1, nx):
-                for i in many:
-                    b = bufs[i][0]
-                    arrived(i, (c, xs[e], zs[d]))
-                    send(i, (c, xs[e], zs[d]), dev(z, x, oc), ag_cs.at[b, e, d])
-        for e in range(nx):
-            for d in range(nz):
-                for i in many:
-                    arrived(i, (oc, xs[e], zs[d]))
-        for copy in started:
-            copy.wait_send()
-
-    def swap_rows():
+                for b, buf in refs(a):
+                    for d in range(nz):
+                        arrived(buf.at[c, xs[e], zs[d]], ag_xr.at[b, xs[e], zs[d]])
+                    send(a, buf.at[c, xs[e]], dev(z, x, oc), ag_cs.at[b, e], ag_cr.at[b, xs[e]])
+
+        def finish(a):
+            for e in range(nx):
+                for b, buf in refs(a):
+                    arrived(buf.at[oc, xs[e]], ag_cr.at[b, xs[e]])
+            for copy in started[a]:
+                copy.wait_send()
+            swap_rows(a)
+
+        return own, along_x, along_core, finish
+
+    def swap_rows(a):
         @pl.loop(0, CORES * nx)
         def _(i):
             cc, xx = i // nx, i % nx
             for zz in range(0, nz, 2):
-                first = xbuf[cc, xx, zz].astype(F32)
-                second = xbuf[cc, xx, zz + 1].astype(F32)
-                xbuf[cc, xx, zz] = jnp.concatenate([first[:ROWS], second[:ROWS]], axis=0).astype(BF16)
-                xbuf[cc, xx, zz + 1] = jnp.concatenate([first[ROWS:], second[ROWS:]], axis=0).astype(BF16)
-
-    def first_projection(depth):
+                first = xbuf[a, cc, xx, zz].astype(F32)
+                second = xbuf[a, cc, xx, zz + 1].astype(F32)
+                xbuf[a, cc, xx, zz] = jnp.concatenate([first[:ROWS], second[:ROWS]], axis=0).astype(BF16)
+                xbuf[a, cc, xx, zz + 1] = jnp.concatenate([first[ROWS:], second[ROWS:]], axis=0).astype(BF16)
+
+    def read_flags(depth):
         meta = mbuf[...].astype(F32).reshape(shards, DEPTHS * ROWS, nblk + BS)
         meta = meta[:, depth * ROWS : (depth + 1) * ROWS, :].reshape(all_rows, nblk + BS)
         mask_v[...] = meta[:, :nblk].astype(BF16)
         if depth == DEPTHS - 1:
             flag_v[...] = meta[:, nblk:]
 
+    def first_projection(depth, a):
+        if depth == 0:
+            win_copy(a).wait()
+
         @pl.loop(0, tiles)
         def _(t):
-            if depth == 0:
-                win_copy(t).wait()
-            pairs = xbuf.reshape(shards // 2, 2, 2 * ROWS, half)
+            col = pl.ds(pl.multiple_of(t * ht, ht), ht)
+            pairs = xbuf.reshape(PARTS, shards // 2, 2, 2 * ROWS, half)
             pre = jnp.dot(
-                pairs[:, 0].reshape(all_rows, half), win_v[t, :half, :], preferred_element_type=F32
+                pairs[a, :, 0].reshape(all_rows, half), win_v[a, :half, col], preferred_element_type=F32
             )
             pre += jnp.dot(
-                pairs[:, 1].reshape(all_rows, half), win_v[t, half:, :], preferred_element_type=F32
+                pairs[a, :, 1].reshape(all_rows, half), win_v[a, half:, col], preferred_element_type=F32
             )
-            col = pl.ds(pl.multiple_of(t * ht, ht), ht)
+            if a > 0:
+                pre += acc[t]
+            if a < PARTS - 1:
+                acc[t] = pre
+                return
             act = jnp.maximum(pre + bin_ref[:, col], 0.0)
             which = lax.broadcasted_iota(jnp.int32, (nblk, ht), 0)
             unit = lax.broadcasted_iota(jnp.int32, (nblk, ht), 1) // BS
@@ -338,23 +364,17 @@
             if last:
                 ver_v[n] = total[:ROWS, SUB:]
 
-        @pl.loop(0, chunks + 3)
+        @pl.loop(0, chunks + LAGS[-1])
         def _(n):
             @pl.when(n < chunks)
             def _():
                 compute(n)
 
-            @pl.when((n >= 1) & (n < chunks + 1))
-            def _():
-                add_core(n - 1)
-
-            @pl.when((n >= 2) & (n < chunks + 2))
-            def _():
-                add_x(n - 2)
-
-            @pl.when(n >= 3)
-            def _():
-                add_z(n - 3)
+            for lag, stage in zip(LAGS, (add_core, add_x, add_z)):
+
+                @pl.when((n >= lag) & (n < chunks + lag))
+                def _():
+                    stage(n - lag)
 
         @pl.loop(0, chunks)
         def _(n):
@@ -369,9 +389,20 @@
     for depth in range(DEPTHS):
         if depth > 0:
             prepare(depth)
-        gather([(0, mbuf), (1, xbuf)] if depth == 0 else [(1, xbuf)])
-        swap_rows()
-        first_projection(depth)
+        own, along_x, along_core, finish = gather_steps(depth)
+        for a in range(PARTS):
+            own(a)
+        along_x(0)
+        along_core(0)
+        for a in range(PARTS):
+            if a + 1 < PARTS:
+                along_x(a + 1)
+            finish(a)
+            if a == 0:
+                read_flags(depth)
+            first_projection(depth, a)
+            if a + 1 < PARTS:
+                along_core(a + 1)
         second_projection(depth)
 
     draft_ref[0] = state_v[...].astype(BF16)
@@ -422,12 +453,13 @@
         in_specs=[vm, vm, vm, vm, vm, vm, vm, hbm, vm, hbm, vm],
         out_specs=(vm, vm),
         scratch_shapes=[
-            pltpu.VMEM((tiles, features, ht), BF16),
+            pltpu.VMEM((PARTS, features // PARTS, width), BF16),
             pltpu.VMEM((SLOTS, width, SUB), BF16),
-            pltpu.VMEM((CORES, nx, nz, 2 * ROWS, features // 2), BF16),
+            pltpu.VMEM((PARTS, CORES, nx, nz, 2 * ROWS, features // PARTS // 2), BF16),
             pltpu.VMEM((CORES, nx, nz, DEPTHS * ROWS, nblk + BS), BF16),
             pltpu.VMEM((rows, nblk), BF16),
             pltpu.VMEM((rows, BS), F32),
+            pltpu.VMEM((tiles, rows, ht), F32),
             pltpu.VMEM((rows + shards, width), BF16),
             pltpu.VMEM((chunks, CORES, nx, nz, 2 * ROWS, SUB + BS), BF16),
             pltpu.VMEM((chunks, nx, nz, 2 * ROWS, SUB + BS), BF16),
@@ -437,12 +469,14 @@
             pltpu.VMEM((ROWS, features), F32),
             pltpu.VMEM((chunks, ROWS, BS), F32),
             pltpu.VMEM((1, features), F32),
-            dma((tiles,)),
+            dma((PARTS,)),
             dma((SLOTS,)),
-            dma((2, CORES, nx, nz)),
-            dma((2, nz)),
-            dma((2, nx, nz)),
-            dma((2, nx, nz)),
+            dma((PARTS + 1, nz)),
+            dma((PARTS + 1, nx, nz)),
+            dma((PARTS + 1, nx)),
+            dma((PARTS + 1, nz)),
+            dma((PARTS + 1, nx, nz)),
+            dma((PARTS + 1, nx)),
             dma((chunks,)),
             dma((chunks,)),
             dma((chunks, nx)),

time: 102 us -> 98.6 us (0.967)
  Pallas kernels: 97.9 us -> 94.2 us
    pallas_call x1, Pallas kernels: 97.9 us -> 94.2 us  [body(): pl.pallas_call(functools.partial(kernel, nz, nx), out_shape=(jax.ShapeDty...]
where the time goes in v2:
time: 98.6 us; the launch traced here: 98.4 us
  Pallas kernels  94.2 us (96%)
  local copies, waits for them, and re-layouts  2.91 us (3%)
  between operations  1.29 us (1%)
    pallas_call x1, Pallas kernels, body(): pl.pallas_call(functools.partial(kernel, nz, nx), out_shape=(jax.ShapeDty...  94.2 us
    unnamed x2, local copies, waits for them, and re-layouts  2.91 us

profile of v2, /device:TPU:0, one launch (start us, length us, event | category | flops | bytes accessed | tf_op | source)
XLA Modules:
  0.0 98.4 jit_solution(13288165642309904648)
XLA Ops:
  1.3 94.2 %shard_map.122 = (bf16[1,8,6144]{2,1,0:T(8,128)(2,1)}, bf16[1,6144]{1,0:T(2,128)(2,1)}) custom-call(bf16[1,8,6144]{2,1,0:T(8,128)(2,1)} %hidden_ref.1, bf16[2,1,8,6144]{3,2,1,0:T(8,128)(2,1)} %embeds_ref.1, s32[2,1,8]{2,1,0:T(1,128)} %parents_ref.1, s32[2,1,8,38]{3,2,1,0:T(8,128)} %active_ref.1, s32[1,1]{1,0:T(1,128)} %bitcast.5.vrow_ref, ...), custom_call_target="tpu_custom_call" | custom-call | flops 19327352832 | bytes 113246208 | tf_op jit(solution)/shard_map/pallas_call | solution.py:447
  95.5 1.5 %copy.16 = bf16[1,8,6144]{2,1,0:T(8,128)(2,1)} copy(bf16[1,8,6144]{2,1,0:T(8,128)(2,1)} %get-tuple-element.4) | data formatting | bytes 196608
  97.0 1.4 %copy.17 = bf16[1,6144]{1,0:T(2,128)(2,1)} copy(bf16[1,6144]{1,0:T(2,128)(2,1)} %get-tuple-element.5) | data formatting | bytes 24576
